TPU v7x, 512 devices: a whole 4x8x8 slice. The times are simulated.
512 devices in a mesh: batch: 32 (over z, x), blk: 16 (over y, core).
Axes of the slice: x: 4, y: 8, z: 8, core: 2. Of those that a mesh axis runs over, the one named last changes fastest.
Arguments:
- points: float32 [1024, 16, 3, 256], P('batch', 'blk'), may hold values from -6 to 6
- centers: float32 [1024, 16, 3, 384], P('batch', 'blk'), may hold values from -6 to 6
- exponents: float32 [1024, 16, 384], P('batch', 'blk'), may hold values from 0.1 to 1
- angular: float32 [1024, 16, 3, 384], P('batch', 'blk'), may hold values from -3 to 3
- grid_weights: float32 [1024, 16, 256], P('batch', 'blk'), may hold values from 0.001 to 0.01
- hartree: float32 [1024, 16, 256], P('batch', 'blk'), may hold values from 0 to 1.7
- load_plan: int32 [16, 1024], P('blk'), may hold values from 0 to 1023, each once within a row
- density_blocks: bfloat16 [256, 128, 128], P('blk'), may hold values from -0.046875 to 0.046875
- pair_lists: int32 [32, 16, 16, 2], P('batch', 'blk'), may hold values from 0 to 15
- batch_pairs: int32 [1024, 16, 9], P('batch', 'blk'), may hold values from 0 to 31, as said below
Outputs:
- hamiltonian: float32 [256, 128, 128], P('blk')
- density: float32 [1024, 16, 256], P('batch', 'blk')
Inputs may be any that keep to these rules, and one draw needn't show every extreme that they name: Each row of load_plan names every storage row of its column once. `pair_lists`: local index of a block pair within the 16 pairs held by one index of blk. `batch_pairs`: entry e of a device's table is the (e % 2)-th block it reads from index e // 2 of blk; every entry of a device's table is named by some pair of its batches.
All inputs are finite; a program needn't handle non-finite values.
Results may differ from a plain program's by a relative error of at most 0.0065.
Values may be sent and summed in bfloat16 or wider, within the bound.
No kernel may reach another device: no remote copies, remote signals or barrier semaphores. Data moves between devices by JAX's collectives and lax.ppermute only.
A program may use at most 64 MiB of HBM per device.

v0:
```python
import jax
import jax.numpy as jnp
from jax import lax
from jax.sharding import PartitionSpec as P

LIST = 3
xc_scale = 0.98474502
soft_square = 0.01


def exchange_potential(grid_rho):
    return -xc_scale * jnp.power(grid_rho * grid_rho + soft_square, 1.0 / 6.0)


def evaluate(points, centers, exponents, angular):
    distance = jnp.zeros(points.shape[:-2] + (points.shape[-1], centers.shape[-1]), jnp.float32)
    angular_part = jnp.ones_like(distance)
    for component in range(3):
        delta = points[..., component, :, None] - centers[..., component, None, :]
        distance = distance + delta * delta
        angular_part = angular_part + angular[..., component, None, :] * delta
    return (jnp.exp(-exponents[..., None, :] * distance) * angular_part).astype(jnp.bfloat16)


def on_device(
    points,
    centers,
    exponents,
    angular,
    grid_weights,
    hartree,
    load_plan,
    density_blocks,
    pair_lists,
    batch_pairs,
):
    slot_count = points.shape[0]
    grid_size = points.shape[3]
    columns = lax.axis_size("blk")
    per_owner = pair_lists.shape[3]
    held_pairs = density_blocks.shape[0]
    block_size = density_blocks.shape[1]
    entries = columns * per_owner
    list_size = LIST
    basis_width = list_size * block_size
    batch_rank = lax.axis_index("batch")
    plan_rows = lax.dynamic_slice_in_dim(load_plan[0], batch_rank * slot_count, slot_count)
    stored = lax.all_gather(hartree[:, 0, :], "batch", axis=0, tiled=True)
    potential = stored[plan_rows]
    wanted = pair_lists[0, 0]
    asked_slots = lax.all_to_all(wanted, "blk", split_axis=0, concat_axis=0, tiled=True)
    owner_base = jnp.arange(entries, dtype=jnp.int32) // per_owner * held_pairs
    global_ids = owner_base + wanted.reshape(entries)
    blank_table = jnp.zeros((entries, block_size, block_size), jnp.bfloat16)
    piece = lax.all_gather(density_blocks, "blk", axis=0, tiled=True)
    inside = (global_ids >= 0) & (global_ids < piece.shape[0])
    chosen = piece[jnp.clip(global_ids, 0, piece.shape[0] - 1)]
    fetched = jnp.where(inside[:, None, None], chosen, blank_table)
    group_size = 4
    loop_turns = slot_count // group_size

    def take_rows(value, turn_index):
        return lax.dynamic_slice_in_dim(value, turn_index * group_size, group_size, 0)

    def integrate(partial_table, turn_index):
        basis = evaluate(
            take_rows(points, turn_index)[:, 0],
            take_rows(centers, turn_index)[:, 0],
            take_rows(exponents, turn_index)[:, 0],
            take_rows(angular, turn_index)[:, 0],
        )
        slot_refs = take_rows(batch_pairs, turn_index)[:, 0]
        blocks = fetched[slot_refs]
        sub_density = (
            blocks.reshape(group_size, list_size, list_size, block_size, block_size)
            .transpose(0, 1, 3, 2, 4)
            .reshape(group_size, basis_width, basis_width)
        )
        inner = jnp.einsum("gpm,gmn->gpn", basis, sub_density, preferred_element_type=jnp.float32)
        grid_rho = jnp.sum(inner * basis.astype(jnp.float32), axis=-1)
        effective = take_rows(potential, turn_index) + exchange_potential(grid_rho)
        weight_rows = take_rows(grid_weights, turn_index)[:, 0]
        scaled = ((weight_rows * effective)[..., None] * basis.astype(jnp.float32)).astype(
            jnp.bfloat16
        )
        full_blocks = jnp.einsum("gpm,gpn->gmn", basis, scaled, preferred_element_type=jnp.float32)
        contributions = (
            full_blocks.reshape(group_size, list_size, block_size, list_size, block_size)
            .transpose(0, 1, 3, 2, 4)
            .reshape(group_size * list_size * list_size, block_size, block_size)
        )
        partial_table = partial_table.at[slot_refs.reshape(-1)].add(contributions)
        return (partial_table, grid_rho)

    zero_table = jnp.zeros((entries, block_size, block_size), jnp.float32)
    partial_table, rho_groups = lax.scan(integrate, zero_table, jnp.arange(loop_turns))
    grid_rho = rho_groups.reshape(slot_count, grid_size)
    received = lax.all_to_all(
        partial_table.reshape(columns, per_owner, block_size, block_size),
        "blk",
        split_axis=0,
        concat_axis=0,
        tiled=True,
    )
    owned_sums = (
        jnp.zeros((held_pairs, block_size, block_size), jnp.float32)
        .at[asked_slots.reshape(entries)]
        .add(received.reshape(entries, block_size, block_size))
    )
    hamiltonian = lax.psum(owned_sums, "batch")
    batch_total = load_plan.shape[1]
    placement = (plan_rows[None, :] == jnp.arange(batch_total, dtype=jnp.int32)[:, None]).astype(
        jnp.float32
    )
    spread_rows = jnp.dot(
        placement, grid_rho, precision=lax.Precision.HIGHEST, preferred_element_type=jnp.float32
    )
    density = lax.psum_scatter(spread_rows, "batch", scatter_dimension=0, tiled=True)
    return (hamiltonian, density[:, None, :])


def solution(mesh):
    return jax.shard_map(
        on_device,
        mesh=mesh,
        in_specs=(
            P("batch", "blk", None, None),
            P("batch", "blk", None, None),
            P("batch", "blk", None),
            P("batch", "blk", None, None),
            P("batch", "blk", None),
            P("batch", "blk", None),
            P("blk", None),
            P("blk", None, None),
            P("batch", "blk", None, None),
            P("batch", "blk", None),
        ),
        out_specs=(P("blk", None, None), P("batch", "blk", None)),
        check_vma=False,
    )
```

profile of v0, /device:TPU:8, one launch (start us, length us, event | category | flops | bytes accessed | tf_op | source)
XLA Modules:
  0.0 800.7 jit_solution(2311108223574678586)
XLA Ops:
  7.2 1.4 copy.57
  9.4 1.3 copy.56
  10.7 9.1 %all-to-all-start = ((s32[16,1,2]{2,1,0:T(1,128)}), s32[16,1,2]{2,1,0:T(1,128)S(1)}, u32[]{:S(2)}, u32[]{:S(2)}) async-start(s32[16,1,2]{2,1,0:T(1,128)} %copy.56), calls=%async_computation | async-start | bytes 16384 | tf_op jit(solution)/shard_map/all_to_all | solution.py:51
  22.3 76.3 %all-gather.6.cloned.1.call-done = f32[1024,1,256]{2,0,1:T(8,128)} async-done(((f32[32,1,256]{2,0,1:T(8,128)}), f32[1024,1,256]{2,0,1:T(8,128)}) %all-gather.6.cloned.1.call-update) | async-done | bytes 1048592 | tf_op jit(solution)/shard_map/all_gather | solution.py:48
  98.6 1.8 gather_fusion.1
  100.4 54.4 %all-gather.4.cloned.1.call-done = bf16[256,128,128]{2,1,0:T(8,128)(2,1)} async-done(((bf16[16,128,128]{2,1,0:T(8,128)(2,1)}), bf16[256,128,128]{2,1,0:T(8,128)(2,1)}) %all-gather.4.cloned.1.call-update) | async-done | bytes 8388624 | tf_op jit(solution)/shard_map/all_gather | solution.py:55
  154.8 4.1 gather_fusion.2
  159.1 1.5 broadcast_in_dim.40
  160.6 234.9 %while.12 = (s32[]{:T(128)}, f32[32,128,128]{2,1,0:T(8,128)}, f32[8,4,256]{2,1,0:T(4,128)S(1)}, s32[8]{0:T(128)S(1)}, s32[32,1,9]{2,0,1:T(8,128)S(1)}, /*index=5...) while((s32[]{:T(128)}, f32[32,128,128]{2,1,0:T(8,128)}, ...), condition=%wide.region_3.4_spmd, body=%wide.region_0.3_spmd.sunk | while | flops 633674496 | bytes 35997664 | solution.py:96
  165.4 1.1 reshape.301
  167.2 2.9 fusion.49
  170.8 4.2 fusion.51
  175.1 3.5 reshape.302
  178.5 1.7 copy.100
  180.3 9.6 %scatter_fusion = f32[32,128,128]{2,1,0:T(8,128)} fusion(f32[32,128,128]{2,1,0:T(8,128)} %get-tuple-element.276, s32[36]{0:T(128)S(1)} %fusion.47, f32[36,128,128]{2,1,0:T(8,128)} %bitcast.106), kind=kCustom, calls=%fused_computation.3.clone.1 | custom fusion | flops 589824 | bytes 7078032 | tf_op jit(solution)/shard_map/while/body/eval_jaxpr/scatter-add | solution.py:92
  194.8 1.1 reshape.301
  196.6 2.9 fusion.49
  200.2 4.2 fusion.51
  204.4 3.5 reshape.302
  207.9 1.7 copy.100
  209.7 9.7 %scatter_fusion = f32[32,128,128]{2,1,0:T(8,128)} fusion(f32[32,128,128]{2,1,0:T(8,128)} %get-tuple-element.276, s32[36]{0:T(128)S(1)} %fusion.47, f32[36,128,128]{2,1,0:T(8,128)} %bitcast.106), kind=kCustom, calls=%fused_computation.3.clone.1 | custom fusion | flops 589824 | bytes 7078032 | tf_op jit(solution)/shard_map/while/body/eval_jaxpr/scatter-add | solution.py:92
  224.2 1.1 reshape.301
  226.0 2.9 fusion.49
  229.6 4.2 fusion.51
  233.8 3.5 reshape.302
  237.3 1.7 copy.100
  239.1 9.7 %scatter_fusion = f32[32,128,128]{2,1,0:T(8,128)} fusion(f32[32,128,128]{2,1,0:T(8,128)} %get-tuple-element.276, s32[36]{0:T(128)S(1)} %fusion.47, f32[36,128,128]{2,1,0:T(8,128)} %bitcast.106), kind=kCustom, calls=%fused_computation.3.clone.1 | custom fusion | flops 589824 | bytes 7078032 | tf_op jit(solution)/shard_map/while/body/eval_jaxpr/scatter-add | solution.py:92
  253.6 1.1 reshape.301
  255.4 2.9 fusion.49
  259.0 4.2 fusion.51
  263.2 3.5 reshape.302
  266.7 1.7 copy.100
  268.5 9.7 %scatter_fusion = f32[32,128,128]{2,1,0:T(8,128)} fusion(f32[32,128,128]{2,1,0:T(8,128)} %get-tuple-element.276, s32[36]{0:T(128)S(1)} %fusion.47, f32[36,128,128]{2,1,0:T(8,128)} %bitcast.106), kind=kCustom, calls=%fused_computation.3.clone.1 | custom fusion | flops 589824 | bytes 7078032 | tf_op jit(solution)/shard_map/while/body/eval_jaxpr/scatter-add | solution.py:92
  283.0 1.1 reshape.301
  284.8 2.9 fusion.49
  288.4 4.2 fusion.51
  292.6 3.5 reshape.302
  296.1 1.7 copy.100
  297.9 9.7 %scatter_fusion = f32[32,128,128]{2,1,0:T(8,128)} fusion(f32[32,128,128]{2,1,0:T(8,128)} %get-tuple-element.276, s32[36]{0:T(128)S(1)} %fusion.47, f32[36,128,128]{2,1,0:T(8,128)} %bitcast.106), kind=kCustom, calls=%fused_computation.3.clone.1 | custom fusion | flops 589824 | bytes 7078032 | tf_op jit(solution)/shard_map/while/body/eval_jaxpr/scatter-add | solution.py:92
  312.4 1.1 reshape.301
  314.2 2.9 fusion.49
  317.8 4.2 fusion.51
  322.0 3.5 reshape.302
  325.5 1.7 copy.100
  327.3 9.6 %scatter_fusion = f32[32,128,128]{2,1,0:T(8,128)} fusion(f32[32,128,128]{2,1,0:T(8,128)} %get-tuple-element.276, s32[36]{0:T(128)S(1)} %fusion.47, f32[36,128,128]{2,1,0:T(8,128)} %bitcast.106), kind=kCustom, calls=%fused_computation.3.clone.1 | custom fusion | flops 589824 | bytes 7078032 | tf_op jit(solution)/shard_map/while/body/eval_jaxpr/scatter-add | solution.py:92
  343.5 2.9 fusion.49
  347.1 4.2 fusion.51
  351.3 3.5 reshape.302
  354.8 1.7 copy.100
  356.6 9.6 %scatter_fusion = f32[32,128,128]{2,1,0:T(8,128)} fusion(f32[32,128,128]{2,1,0:T(8,128)} %get-tuple-element.276, s32[36]{0:T(128)S(1)} %fusion.47, f32[36,128,128]{2,1,0:T(8,128)} %bitcast.106), kind=kCustom, calls=%fused_computation.3.clone.1 | custom fusion | flops 589824 | bytes 7078032 | tf_op jit(solution)/shard_map/while/body/eval_jaxpr/scatter-add | solution.py:92
  371.1 1.1 reshape.301
  372.8 2.9 fusion.49
  376.5 4.2 fusion.51
  380.7 3.5 reshape.302
  384.2 1.7 copy.100
  386.0 9.6 %scatter_fusion = f32[32,128,128]{2,1,0:T(8,128)} fusion(f32[32,128,128]{2,1,0:T(8,128)} %get-tuple-element.276, s32[36]{0:T(128)S(1)} %fusion.47, f32[36,128,128]{2,1,0:T(8,128)} %bitcast.106), kind=kCustom, calls=%fused_computation.3.clone.1 | custom fusion | flops 589824 | bytes 7078032 | tf_op jit(solution)/shard_map/while/body/eval_jaxpr/scatter-add | solution.py:92
  395.5 6.8 all-to-all-start.1
  403.2 1.5 fusion.21
  406.1 43.7 %all-to-all-done.1 = f32[16,2,128,128]{3,2,1,0:T(8,128)S(1)} async-done(((f32[16,2,128,128]{3,2,1,0:T(8,128)}), f32[16,2,128,128]{3,2,1,0:T(8,128)S(1)}, u32[]{:S(2)}, u32[]{:S(2)}) %all-to-all-start.1) | async-done | bytes 2097184 | tf_op jit(solution)/shard_map/all_to_all | solution.py:98
  449.9 2.7 scatter_fusion.1
  453.5 175.6 %reduce-scatter.2.cloned.1.call-done = f32[32,256]{1,0:T(8,128)} async-done(((f32[1024,256]{1,0:T(8,128)}), f32[32,256]{1,0:T(8,128)}) %reduce-scatter.2.cloned.1.call-update) | async-done | bytes 32784 | tf_op jit(solution)/shard_map/reduce_scatter | solution.py:118
  629.1 1.4 copy.66
  630.5 161.3 %all-reduce.2.cloned.1.call-done = f32[16,128,128]{2,1,0:T(8,128)} async-done(((f32[16,128,128]{2,1,0:T(8,128)}), f32[16,128,128]{2,1,0:T(8,128)}) %all-reduce.2.cloned.1.call-update) | async-done | bytes 1048592 | tf_op jit(solution)/shard_map/psum | solution.py:110
  791.8 2.3 copy.114
  (231 shorter events, 52.5 us)
Async XLA Ops:
  7.2 91.4 %all-gather.6.cloned.1.call-start = ((), (), s32[]{:S(2)}) async-start(), calls=%async_computation.6 | async-start | bytes 1081344 | tf_op jit(solution)/shard_map/all_gather | solution.py:48
  8.6 146.2 %all-gather.4.cloned.1.call-start = ((), (), s32[]{:S(2)}) async-start(), calls=%async_computation.3 | async-start | bytes 8912896 | tf_op jit(solution)/shard_map/all_gather | solution.py:55
  10.7 384.8 %all-to-all-start = ((s32[16,1,2]{2,1,0:T(1,128)}), s32[16,1,2]{2,1,0:T(1,128)S(1)}, u32[]{:S(2)}, u32[]{:S(2)}) async-start(s32[16,1,2]{2,1,0:T(1,128)} %copy.56), calls=%async_computation | async-start | bytes 16384 | tf_op jit(solution)/shard_map/all_to_all | solution.py:51
  160.6 3.8 copy-start
  180.3 9.6 %copy-start.1 = (bf16[32,128,128]{2,1,0:T(8,128)(2,1)S(1)}, bf16[32,128,128]{2,1,0:T(8,128)(2,1)}, u32[]{:S(2)}) copy-start(bf16[32,128,128]{2,1,0:T(8,128)(2,1)} %copy-done) | copy-start | bytes 3145732 | tf_op jit(solution)/shard_map/while
  190.0 3.8 copy-start
  209.7 9.7 %copy-start.1 = (bf16[32,128,128]{2,1,0:T(8,128)(2,1)S(1)}, bf16[32,128,128]{2,1,0:T(8,128)(2,1)}, u32[]{:S(2)}) copy-start(bf16[32,128,128]{2,1,0:T(8,128)(2,1)} %copy-done) | copy-start | bytes 3145732 | tf_op jit(solution)/shard_map/while
  219.4 3.8 copy-start
  239.1 9.7 %copy-start.1 = (bf16[32,128,128]{2,1,0:T(8,128)(2,1)S(1)}, bf16[32,128,128]{2,1,0:T(8,128)(2,1)}, u32[]{:S(2)}) copy-start(bf16[32,128,128]{2,1,0:T(8,128)(2,1)} %copy-done) | copy-start | bytes 3145732 | tf_op jit(solution)/shard_map/while
  248.8 3.8 copy-start
  268.5 9.8 %copy-start.1 = (bf16[32,128,128]{2,1,0:T(8,128)(2,1)S(1)}, bf16[32,128,128]{2,1,0:T(8,128)(2,1)}, u32[]{:S(2)}) copy-start(bf16[32,128,128]{2,1,0:T(8,128)(2,1)} %copy-done) | copy-start | bytes 3145732 | tf_op jit(solution)/shard_map/while
  278.2 3.8 copy-start
  297.9 9.7 %copy-start.1 = (bf16[32,128,128]{2,1,0:T(8,128)(2,1)S(1)}, bf16[32,128,128]{2,1,0:T(8,128)(2,1)}, u32[]{:S(2)}) copy-start(bf16[32,128,128]{2,1,0:T(8,128)(2,1)} %copy-done) | copy-start | bytes 3145732 | tf_op jit(solution)/shard_map/while
  307.6 3.8 copy-start
  327.3 9.6 %copy-start.1 = (bf16[32,128,128]{2,1,0:T(8,128)(2,1)S(1)}, bf16[32,128,128]{2,1,0:T(8,128)(2,1)}, u32[]{:S(2)}) copy-start(bf16[32,128,128]{2,1,0:T(8,128)(2,1)} %copy-done) | copy-start | bytes 3145732 | tf_op jit(solution)/shard_map/while
  336.9 3.8 copy-start
  356.6 9.6 %copy-start.1 = (bf16[32,128,128]{2,1,0:T(8,128)(2,1)S(1)}, bf16[32,128,128]{2,1,0:T(8,128)(2,1)}, u32[]{:S(2)}) copy-start(bf16[32,128,128]{2,1,0:T(8,128)(2,1)} %copy-done) | copy-start | bytes 3145732 | tf_op jit(solution)/shard_map/while
  366.3 3.8 copy-start
  386.0 9.6 %copy-start.1 = (bf16[32,128,128]{2,1,0:T(8,128)(2,1)S(1)}, bf16[32,128,128]{2,1,0:T(8,128)(2,1)}, u32[]{:S(2)}) copy-start(bf16[32,128,128]{2,1,0:T(8,128)(2,1)} %copy-done) | copy-start | bytes 3145732 | tf_op jit(solution)/shard_map/while
  395.5 54.2 %all-to-all-start.1 = ((f32[16,2,128,128]{3,2,1,0:T(8,128)}), f32[16,2,128,128]{3,2,1,0:T(8,128)S(1)}, u32[]{:S(2)}, u32[]{:S(2)}) async-start(f32[16,2,128,128]{3,2,1,0:T(8,128)} %bitcast.108), calls=%async_computation.1 | async-start | bytes 4194304 | tf_op jit(solution)/shard_map/all_to_all | solution.py:98
  402.4 226.8 %reduce-scatter.2.cloned.1.call-start = ((), (), s32[]{:S(2)}) async-start(), calls=%async_computation.5 | async-start | bytes 1081344 | tf_op jit(solution)/shard_map/reduce_scatter | solution.py:118
  404.7 387.1 %all-reduce.2.cloned.1.call-start = ((), (), s32[]{:S(2)}) async-start(), calls=%async_computation.4 | async-start | bytes 2097152 | tf_op jit(solution)/shard_map/psum | solution.py:110
  452.5 1.0 copy-start.2
Sparse Core Ops, SparseCore 0:
  11.7 86.7 all-gather.5
  100.7 54.0 all-gather.3
  407.6 221.4 reduce-scatter.1
  633.0 158.7 all-reduce.1
where the time goes:
time: 804 us; the launch traced here: 801 us
  waiting for transfers between devices  512 us (64%)
  local copies, waits for them, and re-layouts  112 us (14%)
  other arithmetic  81.9 us (10%)
  matrix products  58.4 us (7%)
  starting transfers between devices  16.1 us (2%)
  between operations  13.9 us (2%)
    reduce_scatter x1, waiting for transfers between devices, on_device(): lax.psum_scatter(spread_rows, 'batch', scatter_dimension=0, tiled=True)  176 us
    psum x1, waiting for transfers between devices, on_device(): hamiltonian = lax.psum(owned_sums, 'batch')  161 us
    scatter-add x8, other arithmetic, integrate(): partial_table = partial_table.at[slot_refs.reshape(-1)].add(contributions)  77.2 us
    all_gather x1, waiting for transfers between devices, on_device(): stored = lax.all_gather(hartree[:, 0, :], 'batch', axis=0, tiled=True)  76.3 us
    all_gather x1, waiting for transfers between devices, on_device(): piece = lax.all_gather(density_blocks, 'blk', axis=0, tiled=True)  54.4 us
    all_to_all x1, waiting for transfers between devices, on_device(): lax.all_to_all(partial_table.reshape(columns, per_owner, block_size, bloc...  43.7 us
    dot_general x8, matrix products, integrate(): jnp.einsum('gpm,gpn->gmn', basis, scaled, preferred_element_type=jnp.floa...  33.7 us
    reshape x8, local copies, waits for them, and re-layouts, integrate(): full_blocks.reshape(group_size, list_size, block_size, list_size, block_s...  27.7 us
  transfers between devices with their start and end apart: 6, of which 5 were waited for; matrix products, arithmetic and copies ran while one was open for 31% of the time, Pallas kernels for 0%

commit v1 on v0

--- a/solution.py
+++ b/solution.py
@@ -107,7 +107,7 @@
         .at[asked_slots.reshape(entries)]
         .add(received.reshape(entries, block_size, block_size))
     )
-    hamiltonian = lax.psum(owned_sums, "batch")
+    hamiltonian = jnp.sum(lax.all_gather(owned_sums, "batch"), axis=0)
     batch_total = load_plan.shape[1]
     placement = (plan_rows[None, :] == jnp.arange(batch_total, dtype=jnp.int32)[:, None]).astype(
         jnp.float32

time: 804 us -> 893 us (1.11)
  the two profiles are of different devices: /device:TPU:8 before, /device:TPU:1 now
where the time goes in v1:
time: 893 us; the launch traced here: 890 us
  waiting for transfers between devices  592 us (66%)
  local copies, waits for them, and re-layouts  110 us (12%)
  other arithmetic  94.8 us (11%)
  matrix products  58.4 us (7%)
  starting transfers between devices  15.2 us (2%)
  between operations  13.9 us (2%)
    all_gather x1, waiting for transfers between devices, on_device(): hamiltonian = jnp.sum(lax.all_gather(owned_sums, 'batch'), axis=0)  244 us
    reduce_scatter x1, waiting for transfers between devices, on_device(): lax.psum_scatter(spread_rows, 'batch', scatter_dimension=0, tiled=True)  169 us
    scatter-add x8, other arithmetic, integrate(): partial_table = partial_table.at[slot_refs.reshape(-1)].add(contributions)  77.4 us
    all_gather x1, waiting for transfers between devices, on_device(): stored = lax.all_gather(hartree[:, 0, :], 'batch', axis=0, tiled=True)  71.7 us
    all_gather x1, waiting for transfers between devices, on_device(): piece = lax.all_gather(density_blocks, 'blk', axis=0, tiled=True)  60.7 us
    all_to_all x1, waiting for transfers between devices, on_device(): lax.all_to_all(partial_table.reshape(columns, per_owner, block_size, bloc...  45.3 us
    dot_general x8, matrix products, integrate(): jnp.einsum('gpm,gpn->gmn', basis, scaled, preferred_element_type=jnp.floa...  33.7 us
    reshape x8, local copies, waits for them, and re-layouts, integrate(): full_blocks.reshape(group_size, list_size, block_size, list_size, block_s...  27.7 us
  transfers between devices with their start and end apart: 6, of which 5 were waited for; matrix products, arithmetic and copies ran while one was open for 28% of the time, Pallas kernels for 0%

profile of v1, /device:TPU:1, one launch (start us, length us, event | category | flops | bytes accessed | tf_op | source)
XLA Modules:
  0.0 889.9 jit_solution(10053402453071526069)
XLA Ops:
  7.2 1.4 copy.57
  9.4 1.3 copy.56
  10.7 10.2 %all-to-all-start = ((s32[16,1,2]{2,1,0:T(1,128)}), s32[16,1,2]{2,1,0:T(1,128)S(1)}, u32[]{:S(2)}, u32[]{:S(2)}) async-start(s32[16,1,2]{2,1,0:T(1,128)} %copy.56), calls=%async_computation | async-start | bytes 16384 | tf_op jit(solution)/shard_map/all_to_all | solution.py:51
  23.4 71.7 %all-gather.8.cloned.1.call-done = f32[1024,1,256]{2,0,1:T(8,128)} async-done(((f32[32,1,256]{2,0,1:T(8,128)}), f32[1024,1,256]{2,0,1:T(8,128)}) %all-gather.8.cloned.1.call-update) | async-done | bytes 1048592 | tf_op jit(solution)/shard_map/all_gather | solution.py:48
  95.1 1.8 gather_fusion.1
  96.9 60.7 %all-gather.6.cloned.1.call-done = bf16[256,128,128]{2,1,0:T(8,128)(2,1)} async-done(((bf16[16,128,128]{2,1,0:T(8,128)(2,1)}), bf16[256,128,128]{2,1,0:T(8,128)(2,1)}) %all-gather.6.cloned.1.call-update) | async-done | bytes 8388624 | tf_op jit(solution)/shard_map/all_gather | solution.py:55
  157.6 4.1 gather_fusion.2
  161.9 1.5 broadcast_in_dim.40
  163.4 235.1 %while.12 = (s32[]{:T(128)}, f32[32,128,128]{2,1,0:T(8,128)}, f32[8,4,256]{2,1,0:T(4,128)S(1)}, s32[8]{0:T(128)S(1)}, s32[32,1,9]{2,0,1:T(8,128)S(1)}, /*index=5...) while((s32[]{:T(128)}, f32[32,128,128]{2,1,0:T(8,128)}, ...), condition=%wide.region_3.4_spmd, body=%wide.region_0.3_spmd.sunk | while | flops 633674496 | bytes 35997664 | solution.py:96
  168.2 1.1 reshape.302
  170.0 2.9 fusion.49
  173.6 4.2 fusion.51
  177.8 3.5 reshape.303
  181.3 1.7 copy.100
  183.1 9.7 %scatter_fusion = f32[32,128,128]{2,1,0:T(8,128)} fusion(f32[32,128,128]{2,1,0:T(8,128)} %get-tuple-element.276, s32[36]{0:T(128)S(1)} %fusion.47, f32[36,128,128]{2,1,0:T(8,128)} %bitcast.107), kind=kCustom, calls=%fused_computation.3.clone.1 | custom fusion | flops 589824 | bytes 7078032 | tf_op jit(solution)/shard_map/while/body/eval_jaxpr/scatter-add | solution.py:92
  197.6 1.1 reshape.302
  199.4 2.9 fusion.49
  203.0 4.2 fusion.51
  207.3 3.5 reshape.303
  210.7 1.7 copy.100
  212.5 9.7 %scatter_fusion = f32[32,128,128]{2,1,0:T(8,128)} fusion(f32[32,128,128]{2,1,0:T(8,128)} %get-tuple-element.276, s32[36]{0:T(128)S(1)} %fusion.47, f32[36,128,128]{2,1,0:T(8,128)} %bitcast.107), kind=kCustom, calls=%fused_computation.3.clone.1 | custom fusion | flops 589824 | bytes 7078032 | tf_op jit(solution)/shard_map/while/body/eval_jaxpr/scatter-add | solution.py:92
  227.0 1.1 reshape.302
  228.8 2.9 fusion.49
  232.4 4.2 fusion.51
  236.7 3.5 reshape.303
  240.1 1.7 copy.100
  241.9 9.7 %scatter_fusion = f32[32,128,128]{2,1,0:T(8,128)} fusion(f32[32,128,128]{2,1,0:T(8,128)} %get-tuple-element.276, s32[36]{0:T(128)S(1)} %fusion.47, f32[36,128,128]{2,1,0:T(8,128)} %bitcast.107), kind=kCustom, calls=%fused_computation.3.clone.1 | custom fusion | flops 589824 | bytes 7078032 | tf_op jit(solution)/shard_map/while/body/eval_jaxpr/scatter-add | solution.py:92
  256.5 1.1 reshape.302
  258.2 2.9 fusion.49
  261.9 4.2 fusion.51
  266.1 3.5 reshape.303
  269.6 1.7 copy.100
  271.4 9.6 %scatter_fusion = f32[32,128,128]{2,1,0:T(8,128)} fusion(f32[32,128,128]{2,1,0:T(8,128)} %get-tuple-element.276, s32[36]{0:T(128)S(1)} %fusion.47, f32[36,128,128]{2,1,0:T(8,128)} %bitcast.107), kind=kCustom, calls=%fused_computation.3.clone.1 | custom fusion | flops 589824 | bytes 7078032 | tf_op jit(solution)/shard_map/while/body/eval_jaxpr/scatter-add | solution.py:92
  285.8 1.1 reshape.302
  287.6 2.9 fusion.49
  291.2 4.2 fusion.51
  295.4 3.5 reshape.303
  298.9 1.7 copy.100
  300.7 9.6 %scatter_fusion = f32[32,128,128]{2,1,0:T(8,128)} fusion(f32[32,128,128]{2,1,0:T(8,128)} %get-tuple-element.276, s32[36]{0:T(128)S(1)} %fusion.47, f32[36,128,128]{2,1,0:T(8,128)} %bitcast.107), kind=kCustom, calls=%fused_computation.3.clone.1 | custom fusion | flops 589824 | bytes 7078032 | tf_op jit(solution)/shard_map/while/body/eval_jaxpr/scatter-add | solution.py:92
  315.1 1.1 reshape.302
  316.9 2.9 fusion.49
  320.5 4.2 fusion.51
  324.8 3.5 reshape.303
  328.2 1.7 copy.100
  330.0 9.7 %scatter_fusion = f32[32,128,128]{2,1,0:T(8,128)} fusion(f32[32,128,128]{2,1,0:T(8,128)} %get-tuple-element.276, s32[36]{0:T(128)S(1)} %fusion.47, f32[36,128,128]{2,1,0:T(8,128)} %bitcast.107), kind=kCustom, calls=%fused_computation.3.clone.1 | custom fusion | flops 589824 | bytes 7078032 | tf_op jit(solution)/shard_map/while/body/eval_jaxpr/scatter-add | solution.py:92
  344.5 1.1 reshape.302
  346.3 2.9 fusion.49
  349.9 4.2 fusion.51
  354.2 3.5 reshape.303
  357.6 1.7 copy.100
  359.4 9.6 %scatter_fusion = f32[32,128,128]{2,1,0:T(8,128)} fusion(f32[32,128,128]{2,1,0:T(8,128)} %get-tuple-element.276, s32[36]{0:T(128)S(1)} %fusion.47, f32[36,128,128]{2,1,0:T(8,128)} %bitcast.107), kind=kCustom, calls=%fused_computation.3.clone.1 | custom fusion | flops 589824 | bytes 7078032 | tf_op jit(solution)/shard_map/while/body/eval_jaxpr/scatter-add | solution.py:92
  375.6 2.9 fusion.49
  379.2 4.2 fusion.51
  383.5 3.5 reshape.303
  386.9 1.7 copy.100
  388.7 9.8 %scatter_fusion = f32[32,128,128]{2,1,0:T(8,128)} fusion(f32[32,128,128]{2,1,0:T(8,128)} %get-tuple-element.276, s32[36]{0:T(128)S(1)} %fusion.47, f32[36,128,128]{2,1,0:T(8,128)} %bitcast.107), kind=kCustom, calls=%fused_computation.3.clone.1 | custom fusion | flops 589824 | bytes 7078032 | tf_op jit(solution)/shard_map/while/body/eval_jaxpr/scatter-add | solution.py:92
  398.5 4.9 all-to-all-start.1
  404.2 1.5 fusion.21
  407.1 45.3 %all-to-all-done.1 = f32[16,2,128,128]{3,2,1,0:T(8,128)S(1)} async-done(((f32[16,2,128,128]{3,2,1,0:T(8,128)}), f32[16,2,128,128]{3,2,1,0:T(8,128)S(1)}, u32[]{:S(2)}, u32[]{:S(2)}) %all-to-all-start.1) | async-done | bytes 2097184 | tf_op jit(solution)/shard_map/all_to_all | solution.py:98
  452.4 2.7 scatter_fusion.1
  456.1 168.7 %reduce-scatter.2.cloned.1.call-done = f32[32,256]{1,0:T(8,128)} async-done(((f32[1024,256]{1,0:T(8,128)}), f32[32,256]{1,0:T(8,128)}) %reduce-scatter.2.cloned.1.call-update) | async-done | bytes 32784 | tf_op jit(solution)/shard_map/reduce_scatter | solution.py:118
  624.8 1.4 copy.66
  626.2 244.5 %all-gather.10.cloned.1.call-done = f32[512,128,128]{2,1,0:T(8,128)} async-done(((f32[16,128,128]{2,1,0:T(8,128)}), f32[512,128,128]{2,1,0:T(8,128)}) %all-gather.10.cloned.1.call-update) | async-done | bytes 33554448 | tf_op jit(solution)/shard_map/all_gather | solution.py:110
  870.7 12.7 %reduce_sum.18 = f32[16,128,128]{2,1,0:T(8,128)} reduce(f32[32,16,128,128]{3,2,1,0:T(8,128)} %bitcast.111, f32[]{:T(128)} %constant.32.clone.1), dimensions={0}, to_apply=%region_5.6 | reduce | flops 8126464 | bytes 34603012 | tf_op jit(solution)/shard_map/reduce_sum | solution.py:110
  (231 shorter events, 52.4 us)
Async XLA Ops:
  7.2 87.9 %all-gather.8.cloned.1.call-start = ((), (), s32[]{:S(2)}) async-start(), calls=%async_computation.5 | async-start | bytes 1081344 | tf_op jit(solution)/shard_map/all_gather | solution.py:48
  8.6 149.0 %all-gather.6.cloned.1.call-start = ((), (), s32[]{:S(2)}) async-start(), calls=%async_computation.3 | async-start | bytes 8912896 | tf_op jit(solution)/shard_map/all_gather | solution.py:55
  10.7 387.8 %all-to-all-start = ((s32[16,1,2]{2,1,0:T(1,128)}), s32[16,1,2]{2,1,0:T(1,128)S(1)}, u32[]{:S(2)}, u32[]{:S(2)}) async-start(s32[16,1,2]{2,1,0:T(1,128)} %copy.56), calls=%async_computation | async-start | bytes 16384 | tf_op jit(solution)/shard_map/all_to_all | solution.py:51
  163.4 3.8 copy-start
  183.1 9.7 %copy-start.1 = (bf16[32,128,128]{2,1,0:T(8,128)(2,1)S(1)}, bf16[32,128,128]{2,1,0:T(8,128)(2,1)}, u32[]{:S(2)}) copy-start(bf16[32,128,128]{2,1,0:T(8,128)(2,1)} %copy-done) | copy-start | bytes 3145732 | tf_op jit(solution)/shard_map/while
  192.8 3.8 copy-start
  212.5 9.7 %copy-start.1 = (bf16[32,128,128]{2,1,0:T(8,128)(2,1)S(1)}, bf16[32,128,128]{2,1,0:T(8,128)(2,1)}, u32[]{:S(2)}) copy-start(bf16[32,128,128]{2,1,0:T(8,128)(2,1)} %copy-done) | copy-start | bytes 3145732 | tf_op jit(solution)/shard_map/while
  222.2 3.8 copy-start
  241.9 9.7 %copy-start.1 = (bf16[32,128,128]{2,1,0:T(8,128)(2,1)S(1)}, bf16[32,128,128]{2,1,0:T(8,128)(2,1)}, u32[]{:S(2)}) copy-start(bf16[32,128,128]{2,1,0:T(8,128)(2,1)} %copy-done) | copy-start | bytes 3145732 | tf_op jit(solution)/shard_map/while
  251.7 3.8 copy-start
  271.4 9.6 %copy-start.1 = (bf16[32,128,128]{2,1,0:T(8,128)(2,1)S(1)}, bf16[32,128,128]{2,1,0:T(8,128)(2,1)}, u32[]{:S(2)}) copy-start(bf16[32,128,128]{2,1,0:T(8,128)(2,1)} %copy-done) | copy-start | bytes 3145732 | tf_op jit(solution)/shard_map/while
  281.0 3.8 copy-start
  300.7 9.6 %copy-start.1 = (bf16[32,128,128]{2,1,0:T(8,128)(2,1)S(1)}, bf16[32,128,128]{2,1,0:T(8,128)(2,1)}, u32[]{:S(2)}) copy-start(bf16[32,128,128]{2,1,0:T(8,128)(2,1)} %copy-done) | copy-start | bytes 3145732 | tf_op jit(solution)/shard_map/while
  310.3 3.8 copy-start
  330.0 9.7 %copy-start.1 = (bf16[32,128,128]{2,1,0:T(8,128)(2,1)S(1)}, bf16[32,128,128]{2,1,0:T(8,128)(2,1)}, u32[]{:S(2)}) copy-start(bf16[32,128,128]{2,1,0:T(8,128)(2,1)} %copy-done) | copy-start | bytes 3145732 | tf_op jit(solution)/shard_map/while
  339.7 3.8 copy-start
  359.4 9.6 %copy-start.1 = (bf16[32,128,128]{2,1,0:T(8,128)(2,1)S(1)}, bf16[32,128,128]{2,1,0:T(8,128)(2,1)}, u32[]{:S(2)}) copy-start(bf16[32,128,128]{2,1,0:T(8,128)(2,1)} %copy-done) | copy-start | bytes 3145732 | tf_op jit(solution)/shard_map/while
  369.0 3.8 copy-start
  388.7 9.8 %copy-start.1 = (bf16[32,128,128]{2,1,0:T(8,128)(2,1)S(1)}, bf16[32,128,128]{2,1,0:T(8,128)(2,1)}, u32[]{:S(2)}) copy-start(bf16[32,128,128]{2,1,0:T(8,128)(2,1)} %copy-done) | copy-start | bytes 3145732 | tf_op jit(solution)/shard_map/while
  398.5 53.8 %all-to-all-start.1 = ((f32[16,2,128,128]{3,2,1,0:T(8,128)}), f32[16,2,128,128]{3,2,1,0:T(8,128)S(1)}, u32[]{:S(2)}, u32[]{:S(2)}) async-start(f32[16,2,128,128]{3,2,1,0:T(8,128)} %bitcast.109), calls=%async_computation.1 | async-start | bytes 4194304 | tf_op jit(solution)/shard_map/all_to_all | solution.py:98
  403.4 221.4 %reduce-scatter.2.cloned.1.call-start = ((), (), s32[]{:S(2)}) async-start(), calls=%async_computation.4 | async-start | bytes 1081344 | tf_op jit(solution)/shard_map/reduce_scatter | solution.py:118
  405.7 465.0 %all-gather.10.cloned.1.call-start = ((), (), s32[]{:S(2)}) async-start(), calls=%async_computation.6 | async-start | bytes 34603008 | tf_op jit(solution)/shard_map/all_gather | solution.py:110
  455.1 1.0 copy-start.2
Sparse Core Ops, SparseCore 0:
  11.7 83.2 all-gather.7
  97.2 60.3 all-gather.5
  408.6 216.1 reduce-scatter.1
  628.4 242.2 all-gather.9
